TPU v7x, 32 devices: a whole 2x2x4 slice. The times are simulated.
32 devices in a mesh: inp: 4 (over y, core), dep: 2 (over x), out: 4 (over z).
Axes of the slice: x: 2, y: 2, z: 4, core: 2. Of those that a mesh axis runs over, the one named last changes fastest.
Arguments:
- tokens: bfloat16 [1024, 16384], P('inp', 'out'), may hold values from -6 to 6
- gate_up_weight: bfloat16 [16384, 2, 28672], P('out', None, ('inp', 'dep')), may hold values from -0.046875 to 0.046875
- down_weight: bfloat16 [28672, 16384], P(('inp', 'dep'), 'out'), may hold values from -0.03125 to 0.03125
Outputs:
- layer_output: bfloat16 [1024, 16384], P(('inp', 'dep'), 'out')
All inputs are finite; a program needn't handle non-finite values.
Results may differ from a plain program's by a relative error of at most 0.0049.
Values may be sent and summed in bfloat16 or wider, within the bound.
No kernel may reach another device: no remote copies, remote signals or barrier semaphores. Data moves between devices by JAX's collectives and lax.ppermute only.
A program may use at most 320 MiB of HBM per device.

v0:
```python
import jax
import jax.numpy as jnp
from jax import lax
from jax.sharding import PartitionSpec as P


def swiglu(projected):
    return (jax.nn.silu(projected[:, 0, :]) * projected[:, 1, :]).astype(jnp.bfloat16)


def shards(tokens, gate_up_weight, down_weight):
    local_width = gate_up_weight.shape[0]
    block_units = gate_up_weight.shape[2]
    flat_weight = gate_up_weight.reshape(local_width, 2 * block_units)
    projected = jnp.dot(
        lax.all_gather(tokens, "inp", axis=0, tiled=True),
        flat_weight,
        preferred_element_type=jnp.float32,
    )
    projected = projected.reshape(projected.shape[0], 2, block_units)
    totals = lax.psum(projected, "out")
    full_hidden = swiglu(totals)
    result = lax.psum_scatter(
        jnp.dot(full_hidden, down_weight, preferred_element_type=jnp.float32),
        ("inp", "dep"),
        scatter_dimension=0,
        tiled=True,
    )
    return result.astype(jnp.bfloat16)


def solution(mesh):
    placed = (P("inp", "out"), P("out", None, ("inp", "dep")), P(("inp", "dep"), "out"))
    return jax.shard_map(
        shards, mesh=mesh, in_specs=placed, out_specs=P(("inp", "dep"), "out"), check_vma=False
    )
```

profile of v0, /device:TPU:0, one launch (start us, length us, event | category | flops | bytes accessed | tf_op | source)
XLA Modules:
  0.0 1326.8 jit_solution(3293310670858185689)
XLA Ops:
  6.5 0.0 all-gather.2.cloned.1.call-start
  6.5 0.7 all-gather.2.cloned.1.call-update
  7.3 0.0 all-reduce.2.cloned.1.call-start
  7.3 40.0 %copy.5 = bf16[512,8,2,3584]{3,1,2,0:T(8,128)(2,1)} copy(bf16[512,8,2,3584]{3,2,1,0:T(2,128)(2,1)} %bitcast.23) | data formatting | bytes 117440512
  47.3 69.2 %copy.4 = bf16[7168,4096]{1,0:T(8,128)(2,1)} copy(bf16[7168,4096]{0,1:T(8,128)(2,1)} %bitcast.22) | data formatting | bytes 117440512 | tf_op jit(solution)/shard_map/dot_general | solution.py:15
  116.5 0.0 all-gather.2.cloned.1.call-done
  116.5 69.8 %fusion.2 = f32[1024,2,3584]{2,0,1:T(8,128)} fusion(bf16[2,3584,4096]{2,1,0:T(8,128)(2,1)} %bitcast.24, bf16[1024,4096]{1,0:T(8,128)(2,1)} %all-gather.2.cloned.1.call-done), kind=kOutput, calls=%fused_computation.4 | convolution fusion | flops 60129542144 | bytes 96468992 | tf_op jit(solution)/shard_map/dot_general | solution.py:15
  186.3 0.0 all-reduce.2.cloned.1.call-update
  186.3 0.2 reduce-scatter.2.cloned.1.call-start
  186.6 971.3 %all-reduce.2.cloned.1.call-done = f32[1024,2,3584]{2,0,1:T(8,128)} async-done(((f32[1024,2,3584]{2,0,1:T(8,128)}), f32[1024,2,3584]{2,0,1:T(8,128)}) %all-reduce.2.cloned.1.call-update) | async-done | bytes 29360144 | tf_op jit(solution)/shard_map/psum | solution.py:21
  1157.9 44.7 %fusion.4 = f32[1024,4096]{1,0:T(8,128)} fusion(bf16[3584,4096]{1,0:T(8,128)(2,1)} %param.5, f32[1024,2,3584]{2,0,1:T(8,128)} %all-reduce.2.cloned.1.call-done), kind=kOutput, calls=%fused_computation.6 | convolution fusion | flops 30086791168 | bytes 75497472 | tf_op jit(solution)/shard_map/dot_general | solution.py:24
  1202.6 0.0 reduce-scatter.2.cloned.1.call-update
  1202.6 115.0 %reduce-scatter.2.cloned.1.call-done = f32[128,4096]{1,0:T(8,128)} async-done(((f32[1024,4096]{1,0:T(8,128)}), f32[128,4096]{1,0:T(8,128)}) %reduce-scatter.2.cloned.1.call-update) | async-done | bytes 2097168 | tf_op jit(solution)/shard_map/reduce_scatter | solution.py:23
  1317.6 2.7 convert_element_type.7
Async XLA Ops:
  6.5 110.0 %all-gather.2.cloned.1.call-start = ((), (), s32[]{:S(2)}) async-start(), calls=%async_computation.1 | async-start | bytes 10485760 | tf_op jit(solution)/shard_map/all_gather | solution.py:16
  7.3 1150.6 %all-reduce.2.cloned.1.call-start = ((), (), s32[]{:S(2)}) async-start(), calls=%async_computation.2 | async-start | bytes 58720256 | tf_op jit(solution)/shard_map/psum | solution.py:21
  186.3 1131.3 %reduce-scatter.2.cloned.1.call-start = ((), (), s32[]{:S(2)}) async-start(), calls=%async_computation.3 | async-start | bytes 18874368 | tf_op jit(solution)/shard_map/reduce_scatter | solution.py:23
Sparse Core Ops, SparseCore 0:
  8.9 60.9 all-gather.1
  186.4 971.3 all-reduce.1
  1202.7 114.8 reduce-scatter.1
where the time goes:
time: 1330 us
  waiting for transfers between devices  1090 us (82%)
  matrix products  115 us (9%)
  local copies, waits for them, and re-layouts  109 us (8%)
    psum x1, waiting for transfers between devices, shards(): totals = lax.psum(projected, 'out')  971 us
    reduce_scatter x1, waiting for transfers between devices, shards(): lax.psum_scatter(jnp.dot(full_hidden, down_weight, preferred_element_type...  115 us
    dot_general x1, matrix products, shards(): jnp.dot(lax.all_gather(tokens, 'inp', axis=0, tiled=True), flat_weight, p...  69.8 us
    dot_general x1, local copies, waits for them, and re-layouts, shards(): jnp.dot(lax.all_gather(tokens, 'inp', axis=0, tiled=True), flat_weight, p...  69.2 us
    dot_general x1, matrix products, shards(): jnp.dot(full_hidden, down_weight, preferred_element_type=jnp.float32)  44.7 us
    unnamed x1, local copies, waits for them, and re-layouts  40 us
  transfers between devices with their start and end apart: 3, of which 2 were waited for; matrix products, arithmetic and copies ran while one was open for 8% of the time, Pallas kernels for 0%

commit v1 on v0

v1 whole, which is shorter than its diff:
```python
import functools

import jax
import jax.numpy as jnp
from jax import lax
from jax.experimental import pallas as pl
from jax.experimental.pallas import tpu as pltpu
from jax.sharding import PartitionSpec as P

STAGES = 4
PIECES = 4
LANES = 128
EARLY = 2
SPLITS = 2
VMEM_LIMIT = 16 * 2**20


def pieces_of(units):
    return max(n for n in range(1, PIECES + 1) if units % (LANES * n) == 0)


def flatten_kernel(weight_ref, flat_ref):
    rows, _, units = weight_ref.shape
    part = 32

    @pl.loop(0, rows // part)
    def _(step):
        block = pl.ds(pl.multiple_of(step * part, part), part)
        flat_ref[block, :] = weight_ref[block].reshape(part, 2 * units)


def flatten(weight, c, piece):
    width = weight.shape[0]
    rows = min(512, width)
    return pl.pallas_call(
        flatten_kernel,
        grid=(width // rows,),
        in_specs=[pl.BlockSpec((rows, 2, piece), lambda k: (k, 0, c))],
        out_specs=pl.BlockSpec((rows, 2 * piece), lambda k: (k, 0)),
        out_shape=jax.ShapeDtypeStruct((width, 2 * piece), weight.dtype),
        compiler_params=pltpu.CompilerParams(vmem_limit_bytes=VMEM_LIMIT),
        cost_estimate=pl.CostEstimate(
            flops=0, bytes_accessed=8 * width * piece, transcendentals=0
        ),
    )(weight)


def hop_kernel(side, line, sources, takes, sums, units, piece, names, *refs):
    refs = dict(zip(names, refs))
    here = lax.axis_index("out")
    devices = range(line) if side == 0 else range(line - 1, -1, -1)
    first, last = devices[0], devices[-1]
    own_units = 2 * piece * (sums == "send")
    came_units = 2 * piece * takes["sums"]

    def start(source, target, sem):
        pltpu.make_async_copy(source, target, refs["sems"].at[sem]).start()

    def wait(source, target, sem):
        pltpu.make_async_copy(source, target, refs["sems"].at[sem]).wait()

    rows = refs["total"].shape[0] if sums else 0
    if sums:
        for place, source in enumerate(sources):
            if source is not None:

                @pl.when(here == devices[place])
                def _():
                    start(refs["term%d" % source[0]].at[pl.ds(source[1], rows)], refs["own"], 0)

        if takes["sums"]:
            start(refs["came"].at[:, pl.ds(0, 2 * piece)], refs["running"], 1)
    if units:
        target = refs["sent"].at[:, pl.ds(own_units, piece)]

        @pl.when(here == first)
        def _():
            start(refs["fresh"], target, 2)

        @pl.when(here != first)
        def _():
            if takes["units"]:
                start(refs["came"].at[:, pl.ds(came_units, piece)], target, 2)
            else:
                start(refs["fresh"], target, 2)

    if sums:
        for place, source in enumerate(sources):

            @pl.when(here == devices[place])
            def _():
                if source is None:
                    refs["own"][...] = jnp.zeros_like(refs["own"])
                else:
                    wait(refs["term%d" % source[0]].at[pl.ds(source[1], rows)], refs["own"], 0)

        if takes["sums"]:
            wait(refs["came"].at[:, pl.ds(0, 2 * piece)], refs["running"], 1)

        part = 16

        @pl.loop(0, rows // part)
        def _(step):
            block = pl.ds(pl.multiple_of(step * part, part), part)
            total = refs["own"][block, :]
            if takes["sums"]:
                total = total + refs["running"][block, :].astype(jnp.float32)
            refs["own"][block, :] = total
            refs["total"][block, :] = total.astype(jnp.bfloat16)

        if sums == "send":
            start(refs["total"], refs["sent"].at[:, pl.ds(0, 2 * piece)], 3)
        if "done" in refs:

            @pl.when(here == last)
            def _():
                @pl.loop(0, rows // part)
                def _(step):
                    block = pl.ds(pl.multiple_of(step * part, part), part)
                    gate = refs["own"][block, pl.ds(0, piece)]
                    up = refs["own"][block, pl.ds(piece, piece)]
                    now = gate / (1.0 + jnp.exp(-gate)) * up
                    refs["finished"][block, :] = now.astype(jnp.bfloat16)

                start(refs["finished"], refs["done"], 4)
                wait(refs["finished"], refs["done"], 4)

        if sums == "send":
            wait(refs["total"], refs["sent"].at[:, pl.ds(0, 2 * piece)], 3)
    if units:
        wait(refs["fresh"], refs["sent"].at[:, pl.ds(own_units, piece)], 2)


def hop(side, line, came, fresh, terms, sources, takes, sums, units, done, piece, rows):
    names, inputs, out_names, outputs, scratch_names, scratch = [], [], [], [], [], []
    if came is not None:
        names.append("came")
        inputs.append(came)
    if units:
        names.append("fresh")
        inputs.append(fresh)
    for k, term in enumerate(terms):
        names.append("term%d" % k)
        inputs.append(term)
    width = piece * (2 * (sums == "send") + units)
    if width:
        out_names.append("sent")
        outputs.append(jax.ShapeDtypeStruct((rows, width), jnp.bfloat16))
    if done:
        out_names.append("done")
        outputs.append(jax.ShapeDtypeStruct((rows, piece), jnp.bfloat16))
    if sums:
        scratch_names += ["own", "running", "total", "finished"]
        scratch += [
            pltpu.VMEM((rows, 2 * piece), jnp.float32),
            pltpu.VMEM((rows, 2 * piece), jnp.bfloat16),
            pltpu.VMEM((rows, 2 * piece), jnp.bfloat16),
            pltpu.VMEM((rows, piece), jnp.bfloat16),
        ]
    scratch_names.append("sems")
    scratch.append(pltpu.SemaphoreType.DMA((5,)))
    hbm = pl.BlockSpec(memory_space=pltpu.HBM)
    out = pl.pallas_call(
        functools.partial(
            hop_kernel,
            side,
            line,
            sources,
            takes,
            sums,
            units,
            piece,
            names + out_names + scratch_names,
        ),
        in_specs=[hbm] * len(inputs),
        out_specs=[hbm] * len(outputs),
        out_shape=outputs,
        scratch_shapes=scratch,
        compiler_params=pltpu.CompilerParams(vmem_limit_bytes=VMEM_LIMIT // 2),
        cost_estimate=pl.CostEstimate(
            flops=10 * rows * piece, bytes_accessed=16 * rows * piece, transcendentals=rows * piece
        ),
    )(*inputs)
    out = dict(zip(out_names, out))
    return out.get("sent"), out.get("done")


def pick(entries, position):
    chosen = None
    for place, value in entries:
        chosen = value if chosen is None else jnp.where(position[place], value, chosen)
    return chosen


def halve(terms, axis, size, dim):
    index = lax.axis_index(axis)
    bit = 1
    while bit < size:
        shape = terms.shape
        cut = terms.reshape(*shape[:dim], shape[dim] // 2, 2, *shape[dim + 1 :])
        upper = (index // bit) % 2 == 1
        low = lax.index_in_dim(cut, 0, dim + 1, False)
        high = lax.index_in_dim(cut, 1, dim + 1, False)
        send = jnp.where(upper, low, high).astype(jnp.bfloat16)
        pairs = [(device, device ^ bit) for device in range(size)]
        came = lax.ppermute(send, axis, pairs).astype(jnp.float32)
        terms = jnp.where(upper, high, low) + came
        bit *= 2
    return jnp.squeeze(terms, dim)


def shards(mesh, tokens, gate_up_weight, down_weight):
    line, parts, groups = mesh.shape["out"], mesh.shape["dep"], mesh.shape["inp"]
    owners = groups * parts
    width = tokens.shape[1]
    own_rows = tokens.shape[0] // parts
    stage_rows = own_rows // STAGES
    units = gate_up_weight.shape[2]
    columns = pieces_of(units)
    piece = units // columns
    steps = STAGES * columns
    half = owners * stage_rows // 2
    out_width = down_weight.shape[1]

    here = lax.axis_index("out")
    places = [here == place for place in range(line)]
    hops = [
        [(place, place + 1) for place in range(line - 1)],
        [(place + 1, place) for place in range(line - 1)],
    ]

    split_tokens = tokens.reshape(parts, own_rows, width)
    rows = []
    for stage in range(STAGES):
        own = split_tokens[:, stage * stage_rows : (stage + 1) * stage_rows, :]
        own = own.reshape(parts * stage_rows, width)
        rows.append(lax.all_gather(own, "inp", axis=0, tiled=True))

    def after(value, *others):
        return lax.optimization_barrier((value, *others))[0]

    def term(number, flat, token):
        stage, c = divmod(number, columns)
        x = rows[stage] if token is None else after(rows[stage], token)
        return jnp.dot(x, flat[c], preferred_element_type=jnp.float32)

    early = min(EARLY, columns)
    flat = [flatten(gate_up_weight, c, piece) for c in range(early)]
    terms = [term(0, flat, None)]
    came, takes = [None, None], [dict(sums=False, units=False)] * 2
    fresh = [None, None]
    held = [dict(), dict()]
    delays = [line - 1, line]
    outs, results = [], []

    step = 0
    while len(results) < STAGES:
        work = []
        for side in range(2):
            back = 1 - side
            has_sums = step < steps + line - 1
            sums = "send" if step < steps + line - 2 else "end" if has_sums else ""
            age = step - delays[back]
            sends_units = 0 <= age < steps + line - 2
            if sends_units or sums:
                used, sources = [], [None] * line
                for place in range(line):
                    number = step - place
                    if has_sums and 0 <= number < steps:
                        known = [k for k, other in enumerate(used) if other is terms[number]]
                        if not known:
                            used.append(terms[number])
                        sources[place] = (known[0] if known else len(used) - 1, side * half)
                done = has_sums and step >= line - 1
                sent, mine = hop(
                    side,
                    line,
                    came[side],
                    fresh[back],
                    used,
                    sources,
                    takes[side],
                    sums,
                    sends_units,
                    done,
                    piece,
                    half,
                )
                if done:
                    fresh[side] = mine
            else:
                sent = None
            if sends_units:
                held[back][step] = sent[:, -piece:]
            elif takes[side]["units"]:
                held[back][step] = came[side][:, -piece:]
            came[side] = None
            if sent is not None:
                came[side] = lax.ppermute(sent, "out", hops[side])
                last = sent
            takes[side] = dict(sums=sums == "send", units=sends_units)
        if step + 1 < steps:
            if len(flat) < columns:
                flat.append(flatten(after(gate_up_weight, last), len(flat), piece))
            terms.append(term(step + 1, flat, last))
            work.append(terms[-1])
        stage = len(results)
        number = (stage + 1) * columns - 1
        if step >= number + 2 * line - 1:
            full = []
            for side in range(2):
                chunks = []
                for k in range(number - columns + 1, number + 1):
                    begin = k + delays[side]
                    ordered = places if side else places[::-1]
                    chunks.append(
                        pick([(p, held[side][begin + p]) for p in range(line)], ordered)
                    )
                full.append(jnp.concatenate(chunks, 1))
            full = jnp.concatenate(full, 0)
            final = stage == STAGES - 1
            totals = []
            for k in range(SPLITS):
                cut = slice(k * out_width // SPLITS, (k + 1) * out_width // SPLITS)
                out = jnp.dot(full, down_weight[:, cut], preferred_element_type=jnp.float32)
                work.append(out)
                if final:
                    out = out.reshape(groups, parts, stage_rows, out.shape[1])
                    totals.append(halve(halve(out, "inp", groups, 0), "dep", parts, 0))
                else:
                    totals.append(
                        lax.psum_scatter(out, ("inp", "dep"), scatter_dimension=0, tiled=True)
                    )
            results.append(jnp.concatenate(totals, 1).astype(jnp.bfloat16))
        if work and came[0] is not None:
            came[0] = after(came[0], *work)
        step += 1
    return jnp.concatenate(results, 0)


def solution(mesh):
    placed = (P("inp", "out"), P("out", None, ("inp", "dep")), P(("inp", "dep"), "out"))

    def run(tokens, gate_up_weight, down_weight):
        return shards(mesh, tokens, gate_up_weight, down_weight)

    return jax.shard_map(
        run, mesh=mesh, in_specs=placed, out_specs=P(("inp", "dep"), "out"), check_vma=False
    )
```

time: 1330 us -> 549 us (0.41)
  waiting for transfers between devices: 1090 us -> 88.4 us
  starting transfers between devices: 0.26 us -> 128 us
  local copies, waits for them, and re-layouts: 109 us -> 16.6 us
  Pallas kernels: 0 us -> 76.7 us
  matrix products: 115 us -> 190 us
  other arithmetic: 2.69 us -> 21.9 us
    psum x1 -> x0, waiting for transfers between devices: 971 us -> none  [shards(): totals = lax.psum(projected, 'out')]
    ppermute x0 -> x49, starting transfers between devices: none -> 128 us  [the longest x43 125 us: shards(): came[side] = lax.ppermute(sent, 'out', hops[side])]
    reduce_scatter x1 -> x6, waiting for transfers between devices: 115 us -> 0.77 us  [shards(): lax.psum_scatter(out, ('inp', 'dep'), scatter_dimension=0, tiled=True)]
    ppermute x0 -> x49, waiting for transfers between devices: none -> 85.5 us  [the longest x43 61.3 us: shards(): came[side] = lax.ppermute(sent, 'out', hops[side])]
    pallas_call x0 -> x47, Pallas kernels: none -> 76.7 us  [the longest x4 38.7 us: flatten(): pl.pallas_call(flatten_kernel, grid=(width // rows,), in_specs=[pl.BlockS...]
    dot_general x2 -> x24, matrix products: 115 us -> 190 us  [the longest x16 105 us: term(): return jnp.dot(x, flat[c], preferred_element_type=jnp.float32)]
    dot_general x1 -> x0, local copies, waits for them, and re-layouts: 69.2 us -> none  [shards(): jnp.dot(lax.all_gather(tokens, 'inp', axis=0, tiled=True), flat_weight, p...]
    unnamed x1 -> x172, local copies, waits for them, and re-layouts: 40 us -> 13.7 us
  transfers between devices with their start and end apart: 3 -> 59, of which waited for: 2 -> 21; matrix products, arithmetic and copies ran while one was open for 8% -> 39% of each run, Pallas kernels for 0% -> 14%
where the time goes in v1:
time: 549 us; the launch traced here: 539 us
  matrix products  190 us (35%)
  starting transfers between devices  128 us (23%)
  waiting for transfers between devices  88.4 us (16%)
  Pallas kernels  76.7 us (14%)
  other arithmetic  21.9 us (4%)
  local copies, waits for them, and re-layouts  16.6 us (3%)
  between operations  16.4 us (3%)
    ppermute x43, starting transfers between devices, shards(): came[side] = lax.ppermute(sent, 'out', hops[side])  125 us
    dot_general x16, matrix products, term(): return jnp.dot(x, flat[c], preferred_element_type=jnp.float32)  105 us
    dot_general x8, matrix products, shards(): out = jnp.dot(full, down_weight[:, cut], preferred_element_type=jnp.float32)  84.8 us
    ppermute x43, waiting for transfers between devices, shards(): came[side] = lax.ppermute(sent, 'out', hops[side])  61.3 us
    pallas_call x4, Pallas kernels, flatten(): pl.pallas_call(flatten_kernel, grid=(width // rows,), in_specs=[pl.BlockS...  38.7 us
    pallas_call x43, Pallas kernels, hop(): pl.pallas_call(functools.partial(hop_kernel, side, line, sources, takes,...  38 us
    ppermute x6, waiting for transfers between devices, halve(): came = lax.ppermute(send, axis, pairs).astype(jnp.float32)  24.2 us
    select_n x9, other arithmetic, pick(): jnp.where(position[place], value, chosen)  14.1 us
  transfers between devices with their start and end apart: 59, of which 21 were waited for; matrix products, arithmetic and copies ran while one was open for 39% of the time, Pallas kernels for 14%

profile of v1, /device:TPU:0, one launch (start us, length us, event | category | flops | bytes accessed | tf_op | source)
XLA Modules:
  0.0 538.6 jit_solution(9869652561758855455)
XLA Ops:
  6.5 2.9 fusion.28
  11.6 9.5 %shard_map.37 = bf16[4096,1792]{1,0:T(8,128)(2,1)S(1)} custom-call(bf16[4096,2,3584]{2,1,0:T(2,128)(2,1)} %weight_ref.5), custom_call_target="tpu_custom_call" | custom-call | bytes 29360128 | tf_op jit(solution)/shard_map/pallas_call | solution.py:35
  21.1 5.1 copy-done.28
  26.2 9.5 %shard_map.39 = bf16[4096,1792]{1,0:T(8,128)(2,1)S(1)} custom-call(bf16[4096,2,3584]{2,1,0:T(2,128)(2,1)} %weight_ref.5), custom_call_target="tpu_custom_call" | custom-call | bytes 29360128 | tf_op jit(solution)/shard_map/pallas_call | solution.py:35
  35.7 5.2 copy-done.26
  40.9 9.2 %fusion.29.refs_0_.refs_2_.refs_3_.refs_4_.refs_5_ = f32[256,1792]{1,0:T(8,128)S(1)} fusion(bf16[256,4096]{1,0:T(8,128)(2,1)} %all-gather.5.cloned.1.call-done, bf16[4096,1792]{1,0:T(8,128)(2,1)} %copy-done.28), kind=kOutput, calls=%fused_computation.82 | convolution fusion | flops 3758096384 | bytes 18612224 | tf_op jit(solution)/shard_map/dot_general | solution.py:245
  52.6 5.5 %collective-permute-start.3 = (bf16[128,1792]{1,0:T(8,128)(2,1)S(1)}, bf16[128,1792]{1,0:T(8,128)(2,1)S(1)}, u32[]{:S(2)}, u32[]{:S(2)}) collective-permute-start(bf16[128,1792]{1,0:T(8,128)(2,1)S(1)} %shard_map.43), channel_id=1, source_target_pairs={{0,1},{1,2},{2,3},{4,5},{5,6},{6,7},{8,9},{9,10},{10,11},{12,13},{... | collective-permute-start | bytes 1376264 | tf_op jit(solution)/shard_map/ppermute | solution.py:299
  58.1 4.1 fusion.30.refs_1_.refs_2_.refs_3_.refs_4_.refs_5_
  62.2 9.5 %shard_map.41 = bf16[4096,1792]{1,0:T(8,128)(2,1)S(1)} custom-call(bf16[4096,2,3584]{2,1,0:T(2,128)(2,1)} %weight_ref.5), custom_call_target="tpu_custom_call" | custom-call | bytes 29360128 | tf_op jit(solution)/shard_map/pallas_call | solution.py:35
  74.8 4.6 collective-permute-start.4
  79.4 4.1 fusion.31.refs_1_.refs_2_.refs_3_.refs_4_.refs_5_
  83.5 10.2 %shard_map.46 = bf16[4096,1792]{1,0:T(8,128)(2,1)S(1)} custom-call(bf16[4096,2,3584]{2,1,0:T(2,128)(2,1)} %weight_ref.5), custom_call_target="tpu_custom_call" | custom-call | bytes 29360128 | tf_op jit(solution)/shard_map/pallas_call | solution.py:35
  94.8 3.7 collective-permute-start.5
  101.1 4.1 fusion.32.refs_1_.refs_2_.refs_3_.refs_4_.refs_5_
  108.4 4.1 collective-permute-done.2.refs_0_
  115.1 4.8 collective-permute-start.7
  120.0 8.6 %fusion.33.refs_2_.refs_3_.refs_4_.refs_5_ = f32[256,1792]{1,0:T(8,128)S(1)} fusion(bf16[256,4096]{1,0:T(8,128)(2,1)} %all-gather.7.cloned.1.call-done, bf16[4096,1792]{1,0:T(8,128)(2,1)} %copy-done.28), kind=kOutput, calls=%fused_computation.86 | convolution fusion | flops 3758096384 | bytes 18612224 | tf_op jit(solution)/shard_map/dot_general | solution.py:245
  129.4 3.3 collective-permute-start.9
  135.3 4.1 fusion.34.refs_2_.refs_3_.refs_4_.refs_5_
  139.3 4.9 collective-permute-done.9.refs_0_
  144.8 4.4 collective-permute-start.11
  152.1 8.0 %fusion.35.refs_2_.refs_3_.refs_4_.refs_5_ = f32[256,1792]{1,0:T(8,128)S(1)} fusion(bf16[256,4096]{1,0:T(8,128)(2,1)S(1)} %copy-done.68, bf16[4096,1792]{1,0:T(8,128)(2,1)} %copy-done.25), kind=kOutput, calls=%fused_computation.88 | convolution fusion | flops 3758096384 | bytes 18612224 | tf_op jit(solution)/shard_map/dot_general | solution.py:245
  160.7 4.9 collective-permute-start.13
  168.1 4.1 fusion.36.refs_2_.refs_3_.refs_4_.refs_5_
  176.8 4.4 collective-permute-start.15
  183.9 8.6 %fusion.37.refs_2_.refs_3_.refs_4_.refs_5_ = f32[256,1792]{1,0:T(8,128)S(1)} fusion(bf16[256,4096]{1,0:T(8,128)(2,1)} %all-gather.9.cloned.1.call-done, bf16[4096,1792]{1,0:T(8,128)(2,1)} %copy-done.28), kind=kOutput, calls=%fused_computation.90 | convolution fusion | flops 3758096384 | bytes 18612224 | tf_op jit(solution)/shard_map/dot_general | solution.py:245
  193.1 4.6 collective-permute-start.17
  200.2 8.0 %fusion.38.refs_2_.refs_3_.refs_4_.refs_5_ = f32[256,1792]{1,0:T(8,128)S(1)} fusion(bf16[256,4096]{1,0:T(8,128)(2,1)S(1)} %copy-done.67, bf16[4096,1792]{1,0:T(8,128)(2,1)} %copy-done.26), kind=kOutput, calls=%fused_computation.91 | convolution fusion | flops 3758096384 | bytes 18612224 | tf_op jit(solution)/shard_map/dot_general | solution.py:245
  208.8 5.1 collective-permute-start.18
  216.6 4.1 fusion.39.refs_2_.refs_3_.refs_4_.refs_5_
  225.0 3.1 collective-permute-done.19.refs_0_
  232.4 10.5 %fusion.6 = f32[256,2048]{1,0:T(8,128)} fusion(bf16[3584,4096]{1,0:T(8,128)(2,1)} %param.5, bf16[128,896]{1,0:T(8,128)(2,1)S(1)} %get-tuple-element.226, bf16[128,896]{1,0:T(8,128)(2,1)S(1)} %get-tuple-element.225, bf16[128,896]{1,0:T(8,128)(2,1)S(1)} %get-tuple-element.224, bf16[128,896]{1,0:T(8,128)(2,1)S(1)} %get-tuple-element.223, ...), kind=kOutput, calls=%fused_computation.6 | convolution fusion | flops 3772776448 | bytes 18612224 | tf_op jit(solution)/shard_map/dot_general | solution.py:325
  245.6 12.0 %fusion.14 = f32[256,2048]{1,0:T(8,128)} fusion(bf16[3584,4096]{1,0:T(8,128)(2,1)} %param.5, bf16[128,896]{1,0:T(8,128)(2,1)} %copy-done.54, bf16[128,896]{1,0:T(8,128)(2,1)} %copy-done.53, bf16[128,896]{1,0:T(8,128)(2,1)} %copy-done.52, bf16[128,896]{1,0:T(8,128)(2,1)} %copy-done.51, bf16[128,896]{1,0:T(8,128)(2,1)} %copy-done.59, ...), kind=kOutput, calls=%fused_computation.14 | convolution fusion | flops 3772776448 | bytes 18612224 | tf_op jit(solution)/shard_map/dot_general | solution.py:325
  258.1 8.6 %fusion.40.refs_2_.refs_3_.refs_4_.refs_5_ = f32[256,1792]{1,0:T(8,128)S(1)} fusion(bf16[256,4096]{1,0:T(8,128)(2,1)} %all-gather.9.cloned.1.call-done, bf16[4096,1792]{1,0:T(8,128)(2,1)} %copy-done.24), kind=kOutput, calls=%fused_computation.93 | convolution fusion | flops 3758096384 | bytes 18612224 | tf_op jit(solution)/shard_map/dot_general | solution.py:245
  268.2 4.8 collective-permute-start.23
  275.8 8.6 %fusion.41.refs_2_.refs_3_.refs_4_.refs_5_ = f32[256,1792]{1,0:T(8,128)S(1)} fusion(bf16[256,4096]{1,0:T(8,128)(2,1)} %all-gather.11.cloned.1.call-done, bf16[4096,1792]{1,0:T(8,128)(2,1)} %copy-done.28), kind=kOutput, calls=%fused_computation.94 | convolution fusion | flops 3758096384 | bytes 18612224 | tf_op jit(solution)/shard_map/dot_general | solution.py:245
  285.0 4.6 collective-permute-start.25
  292.0 8.5 %fusion.42.refs_2_.refs_3_.refs_4_ = f32[256,1792]{1,0:T(8,128)S(1)} fusion(bf16[256,4096]{1,0:T(8,128)(2,1)S(1)} %copy-done.66, bf16[4096,1792]{1,0:T(8,128)(2,1)} %copy-done.26), kind=kOutput, calls=%fused_computation.95 | convolution fusion | flops 3758096384 | bytes 18612224 | tf_op jit(solution)/shard_map/dot_general | solution.py:245
  301.1 5.0 collective-permute-start.26
  309.2 4.1 fusion.43.refs_2_.refs_3_
  313.3 4.2 collective-permute-done.26.refs_0_
  318.8 4.8 collective-permute-start.29
  330.9 10.6 %fusion.4 = f32[256,2048]{1,0:T(8,128)} fusion(bf16[3584,4096]{1,0:T(8,128)(2,1)} %param.5, bf16[128,896]{1,0:T(8,128)(2,1)S(1)} %get-tuple-element.222, bf16[128,896]{1,0:T(8,128)(2,1)S(1)} %get-tuple-element.221, bf16[128,896]{1,0:T(8,128)(2,1)S(1)} %get-tuple-element.220, bf16[128,896]{1,0:T(8,128)(2,1)S(1)} %get-tuple-element.219, ...), kind=kOutput, calls=%fused_computation.4 | convolution fusion | flops 3772776448 | bytes 18612224 | tf_op jit(solution)/shard_map/dot_general | solution.py:325
  341.6 11.1 %fusion.12 = f32[256,2048]{1,0:T(8,128)} fusion(bf16[3584,4096]{1,0:T(8,128)(2,1)} %param.5, bf16[128,896]{1,0:T(8,128)(2,1)} %copy-done.58, bf16[128,896]{1,0:T(8,128)(2,1)} %copy-done.57, bf16[128,896]{1,0:T(8,128)(2,1)} %copy-done.56, bf16[128,896]{1,0:T(8,128)(2,1)} %copy-done.55, bf16[128,896]{1,0:T(8,128)(2,1)} %copy-done.62, ...), kind=kOutput, calls=%fused_computation.12 | convolution fusion | flops 3772776448 | bytes 18612224 | tf_op jit(solution)/shard_map/dot_general | solution.py:325
  352.8 8.9 %fusion.44.refs_2_ = f32[256,1792]{1,0:T(8,128)S(1)} fusion(bf16[256,4096]{1,0:T(8,128)(2,1)} %all-gather.11.cloned.1.call-done, bf16[4096,1792]{1,0:T(8,128)(2,1)} %copy-done.24), kind=kOutput, calls=%fused_computation.97 | convolution fusion | flops 3758096384 | bytes 18612224 | tf_op jit(solution)/shard_map/dot_general | solution.py:245
  362.3 4.9 collective-permute-start.31
  369.7 12.1 %collective-permute-done.31.refs_0_ = bf16[128,2688]{1,0:T(8,128)(2,1)S(1)} collective-permute-done((bf16[128,2688]{1,0:T(8,128)(2,1)S(1)}, bf16[128,2688]{1,0:T(8,128)(2,1)S(1)}, u32[]{:S(2)}, u32[]{:S(2)}) %collective-permute-start.31) | collective-permute-done | bytes 688160 | tf_op jit(solution)/shard_map/ppermute | solution.py:299
  382.9 4.6 collective-permute-start.33
  390.2 11.9 %collective-permute-done.33.refs_0_ = bf16[128,2688]{1,0:T(8,128)(2,1)S(1)} collective-permute-done((bf16[128,2688]{1,0:T(8,128)(2,1)}, bf16[128,2688]{1,0:T(8,128)(2,1)S(1)}, u32[]{:S(2)}, u32[]{:S(2)}) %collective-permute-start.33) | collective-permute-done | bytes 688160 | tf_op jit(solution)/shard_map/ppermute | solution.py:299
  404.0 4.3 collective-permute-start.34
  411.1 5.7 %collective-permute-done.34.refs_0_ = bf16[128,2688]{1,0:T(8,128)(2,1)S(1)} collective-permute-done((bf16[128,2688]{1,0:T(8,128)(2,1)S(1)}, bf16[128,2688]{1,0:T(8,128)(2,1)S(1)}, u32[]{:S(2)}, u32[]{:S(2)}) %collective-permute-start.34) | collective-permute-done | bytes 688160 | tf_op jit(solution)/shard_map/ppermute | solution.py:299
  418.9 3.7 collective-permute-done.35.refs_0_
  425.4 10.6 %fusion.2 = f32[256,2048]{1,0:T(8,128)} fusion(bf16[3584,4096]{1,0:T(8,128)(2,1)} %param.5, bf16[128,896]{1,0:T(8,128)(2,1)S(1)} %get-tuple-element.214, bf16[128,896]{1,0:T(8,128)(2,1)S(1)} %get-tuple-element.213, bf16[128,896]{1,0:T(8,128)(2,1)S(1)} %get-tuple-element.212, bf16[128,896]{1,0:T(8,128)(2,1)S(1)} %get-tuple-element.211, ...), kind=kOutput, calls=%fused_computation.2 | convolution fusion | flops 3772776448 | bytes 18612224 | tf_op jit(solution)/shard_map/dot_general | solution.py:325
  436.1 2.5 collective-permute-start.39
  439.9 11.0 %fusion.10 = f32[256,2048]{1,0:T(8,128)} fusion(bf16[3584,4096]{1,0:T(8,128)(2,1)} %param.5, bf16[128,896]{1,0:T(8,128)(2,1)S(1)} %get-tuple-element.214, bf16[128,896]{1,0:T(8,128)(2,1)S(1)} %get-tuple-element.213, bf16[128,896]{1,0:T(8,128)(2,1)S(1)} %get-tuple-element.212, bf16[128,896]{1,0:T(8,128)(2,1)S(1)} %get-tuple-element.211, ...), kind=kOutput, calls=%fused_computation.10 | convolution fusion | flops 3772776448 | bytes 18612224 | tf_op jit(solution)/shard_map/dot_general | solution.py:325
  451.1 4.7 collective-permute-start.40
  457.5 2.5 collective-permute-done.40.refs_0_
  460.3 4.5 collective-permute-start.41
  470.9 5.3 collective-permute-start.42
  480.7 9.2 %fusion.8 = f32[256,2048]{1,0:T(8,128)S(1)} fusion(bf16[3584,4096]{1,0:T(8,128)(2,1)} %param.5, bf16[128,896]{1,0:T(8,128)(2,1)S(1)} %get-tuple-element.232, bf16[128,896]{1,0:T(8,128)(2,1)S(1)} %get-tuple-element.231, bf16[128,896]{1,0:T(8,128)(2,1)S(1)} %get-tuple-element.230, bf16[128,896]{1,0:T(8,128)(2,1)S(1)} %get-tuple-element.229, ...), kind=kOutput, calls=%fused_computation.8 | convolution fusion | flops 3772776448 | bytes 18612224 | tf_op jit(solution)/shard_map/dot_general | solution.py:325
  490.1 9.7 %fusion = f32[256,2048]{1,0:T(8,128)S(1)} fusion(bf16[3584,4096]{1,0:T(8,128)(2,1)} %param.5, bf16[128,896]{1,0:T(8,128)(2,1)S(1)} %get-tuple-element.232, bf16[128,896]{1,0:T(8,128)(2,1)S(1)} %get-tuple-element.231, bf16[128,896]{1,0:T(8,128)(2,1)S(1)} %get-tuple-element.230, bf16[128,896]{1,0:T(8,128)(2,1)S(1)} %get-tuple-element.229, ...), kind=kOutput, calls=%fused_computation | convolution fusion | flops 3772776448 | bytes 18612224 | tf_op jit(solution)/shard_map/dot_general | solution.py:325
  503.1 12.1 %collective-permute-done.44 = bf16[1,2,32,2048]{3,2,1,0:T(8,128)(2,1)S(1)} collective-permute-done((bf16[1,2,32,2048]{3,2,1,0:T(8,128)(2,1)S(1)}, bf16[1,2,32,2048]{3,2,1,0:T(8,128)(2,1)S(1)}, u32[]{:S(2)}, u32[]{:S(2)}) %collective-permute-start.44) | collective-permute-done | bytes 262176 | tf_op jit(solution)/shard_map/ppermute | solution.py:206
  515.4 4.9 collective-permute-done.47
  521.2 6.3 %collective-permute-done.48 = bf16[1,32,2048]{2,1,0:T(8,128)(2,1)S(1)} collective-permute-done((bf16[1,32,2048]{2,1,0:T(8,128)(2,1)S(1)}, bf16[1,32,2048]{2,1,0:T(8,128)(2,1)S(1)}, u32[]{:S(2)}, u32[]{:S(2)}) %collective-permute-start.48) | collective-permute-done | bytes 131104 | tf_op jit(solution)/shard_map/ppermute | solution.py:206
  (340 shorter events, 109.3 us)
Async XLA Ops:
  6.5 34.4 %all-gather.5.cloned.1.call-start = ((), (), s32[]{:S(2)}) async-start(), calls=%async_computation.6 | async-start | bytes 2621440 | tf_op jit(solution)/shard_map/all_gather | solution.py:237
  9.5 105.6 %all-gather.7.cloned.1.call-start = ((), (), s32[]{:S(2)}) async-start(), calls=%async_computation.7 | async-start | bytes 2621440 | tf_op jit(solution)/shard_map/all_gather | solution.py:237
  10.2 173.7 %all-gather.9.cloned.1.call-start = ((), (), s32[]{:S(2)}) async-start(), calls=%async_computation.8 | async-start | bytes 2621440 | tf_op jit(solution)/shard_map/all_gather | solution.py:237
  11.0 264.8 %all-gather.11.cloned.1.call-start = ((), (), s32[]{:S(2)}) async-start(), calls=%async_computation.11 | async-start | bytes 2621440 | tf_op jit(solution)/shard_map/all_gather | solution.py:237
  11.5 455.0 %reduce-scatter.9.cloned.1.call-start = ((), (), s32[]{:S(2)}) async-start(), calls=%async_computation.10 | async-start | bytes 2359296 | tf_op jit(solution)/shard_map/reduce_scatter | solution.py:332
  51.3 20.4 %collective-permute-start = (bf16[128,1792]{1,0:T(8,128)(2,1)S(1)}, bf16[128,1792]{1,0:T(8,128)(2,1)S(1)}, u32[]{:S(2)}, u32[]{:S(2)}) collective-permute-start(bf16[128,1792]{1,0:T(8,128)(2,1)S(1)} %shard_map.38), channel_id=1, source_target_pairs={{1,0},{2,1},{3,2},{5,4},{6,5},{7,6},{9,8},{10,9},{11,10},{13,12},{... | collective-permute-start | bytes 1376264 | tf_op jit(solution)/shard_map/ppermute | solution.py:299
  52.6 21.3 %collective-permute-start.3 = (bf16[128,1792]{1,0:T(8,128)(2,1)S(1)}, bf16[128,1792]{1,0:T(8,128)(2,1)S(1)}, u32[]{:S(2)}, u32[]{:S(2)}) collective-permute-start(bf16[128,1792]{1,0:T(8,128)(2,1)S(1)} %shard_map.43), channel_id=1, source_target_pairs={{0,1},{1,2},{2,3},{4,5},{5,6},{6,7},{8,9},{9,10},{10,11},{12,13},{... | collective-permute-start | bytes 1376264 | tf_op jit(solution)/shard_map/ppermute | solution.py:299
  72.5 25.9 %collective-permute-start.1 = (bf16[128,1792]{1,0:T(8,128)(2,1)S(1)}, bf16[128,1792]{1,0:T(8,128)(2,1)S(1)}, u32[]{:S(2)}, u32[]{:S(2)}) collective-permute-start(bf16[128,1792]{1,0:T(8,128)(2,1)S(1)} %shard_map.40), channel_id=1, source_target_pairs={{1,0},{2,1},{3,2},{5,4},{6,5},{7,6},{9,8},{10,9},{11,10},{13,12},{... | collective-permute-start | bytes 1376264 | tf_op jit(solution)/shard_map/ppermute | solution.py:299
  74.8 18.9 %collective-permute-start.4 = (bf16[128,1792]{1,0:T(8,128)(2,1)S(1)}, bf16[128,1792]{1,0:T(8,128)(2,1)S(1)}, u32[]{:S(2)}, u32[]{:S(2)}) collective-permute-start(bf16[128,1792]{1,0:T(8,128)(2,1)S(1)} %shard_map.44), channel_id=1, source_target_pairs={{0,1},{1,2},{2,3},{4,5},{5,6},{6,7},{8,9},{9,10},{10,11},{12,13},{... | collective-permute-start | bytes 1376264 | tf_op jit(solution)/shard_map/ppermute | solution.py:299
  94.8 12.6 %collective-permute-start.5 = (bf16[128,1792]{1,0:T(8,128)(2,1)S(1)}, bf16[128,1792]{1,0:T(8,128)(2,1)S(1)}, u32[]{:S(2)}, u32[]{:S(2)}) collective-permute-start(bf16[128,1792]{1,0:T(8,128)(2,1)S(1)} %shard_map.45), channel_id=1, source_target_pairs={{0,1},{1,2},{2,3},{4,5},{5,6},{6,7},{8,9},{9,10},{10,11},{12,13},{... | collective-permute-start | bytes 1376264 | tf_op jit(solution)/shard_map/ppermute | solution.py:299
  99.3 13.1 %collective-permute-start.2 = (bf16[128,1792]{1,0:T(8,128)(2,1)S(1)}, bf16[128,1792]{1,0:T(8,128)(2,1)S(1)}, u32[]{:S(2)}, u32[]{:S(2)}) collective-permute-start(bf16[128,1792]{1,0:T(8,128)(2,1)S(1)} %shard_map.42), channel_id=1, source_target_pairs={{1,0},{2,1},{3,2},{5,4},{6,5},{7,6},{9,8},{10,9},{11,10},{13,12},{... | collective-permute-start | bytes 1376264 | tf_op jit(solution)/shard_map/ppermute | solution.py:299
  113.8 19.0 %collective-permute-start.6 = (bf16[128,2688]{1,0:T(8,128)(2,1)S(1)}, bf16[128,2688]{1,0:T(8,128)(2,1)S(1)}, u32[]{:S(2)}, u32[]{:S(2)}) collective-permute-start(bf16[128,2688]{1,0:T(8,128)(2,1)S(1)} %get-tuple-element.111), channel_id=1, source_target_pairs={{1,0},{2,1},{3,2},{5,4},{6,5},{7,6},{9,8},{10,9},{11,10},{13,12},{... | collective-permute-start | bytes 2064392 | tf_op jit(solution)/shard_map/ppermute | solution.py:299
  115.1 13.4 %collective-permute-start.7 = (bf16[128,1792]{1,0:T(8,128)(2,1)}, bf16[128,1792]{1,0:T(8,128)(2,1)S(1)}, u32[]{:S(2)}, u32[]{:S(2)}) collective-permute-start(bf16[128,1792]{1,0:T(8,128)(2,1)} %copy-done.48), channel_id=1, source_target_pairs={{0,1},{1,2},{2,3},{4,5},{5,6},{6,7},{8,9},{9,10},{10,11},{12,13},{... | collective-permute-start | bytes 1376264 | tf_op jit(solution)/shard_map/ppermute | solution.py:299
  129.4 14.8 %collective-permute-start.9 = (bf16[128,2688]{1,0:T(8,128)(2,1)S(1)}, bf16[128,2688]{1,0:T(8,128)(2,1)S(1)}, u32[]{:S(2)}, u32[]{:S(2)}) collective-permute-start(bf16[128,2688]{1,0:T(8,128)(2,1)S(1)} %get-tuple-element.118), channel_id=1, source_target_pairs={{0,1},{1,2},{2,3},{4,5},{5,6},{6,7},{8,9},{9,10},{10,11},{12,13},{... | collective-permute-start | bytes 2064392 | tf_op jit(solution)/shard_map/ppermute | solution.py:299
  133.9 38.3 %copy-start.40 = (bf16[128,2688]{1,0:T(8,128)(2,1)}, bf16[128,2688]{1,0:T(8,128)(2,1)S(1)}, u32[]{:S(2)}) copy-start(bf16[128,2688]{1,0:T(8,128)(2,1)S(1)} %get-tuple-element.117) | copy-start | bytes 2064388
  133.9 15.6 %collective-permute-start.8 = (bf16[128,2688]{1,0:T(8,128)(2,1)S(1)}, bf16[128,2688]{1,0:T(8,128)(2,1)S(1)}, u32[]{:S(2)}, u32[]{:S(2)}) collective-permute-start(bf16[128,2688]{1,0:T(8,128)(2,1)S(1)} %get-tuple-element.117), channel_id=1, source_target_pairs={{1,0},{2,1},{3,2},{5,4},{6,5},{7,6},{9,8},{10,9},{11,10},{13,12},{... | collective-permute-start | bytes 2064392 | tf_op jit(solution)/shard_map/ppermute | solution.py:299
  139.3 41.9 %copy-start.18 = (f32[256,1792]{1,0:T(8,128)}, f32[256,1792]{1,0:T(8,128)S(1)}, u32[]{:S(2)}) copy-start(f32[256,1792]{1,0:T(8,128)S(1)} %fusion.34.refs_2_.refs_3_.refs_4_.refs_5_) | copy-start | bytes 5505028
  144.8 15.4 %collective-permute-start.11 = (bf16[128,2688]{1,0:T(8,128)(2,1)S(1)}, bf16[128,2688]{1,0:T(8,128)(2,1)S(1)}, u32[]{:S(2)}, u32[]{:S(2)}) collective-permute-start(bf16[128,2688]{1,0:T(8,128)(2,1)S(1)} %get-tuple-element.124), channel_id=1, source_target_pairs={{0,1},{1,2},{2,3},{4,5},{5,6},{6,7},{8,9},{9,10},{10,11},{12,13},{... | collective-permute-start | bytes 2064392 | tf_op jit(solution)/shard_map/ppermute | solution.py:299
  150.6 15.0 %collective-permute-start.10 = (bf16[128,2688]{1,0:T(8,128)(2,1)S(1)}, bf16[128,2688]{1,0:T(8,128)(2,1)S(1)}, u32[]{:S(2)}, u32[]{:S(2)}) collective-permute-start(bf16[128,2688]{1,0:T(8,128)(2,1)S(1)} %get-tuple-element.123), channel_id=1, source_target_pairs={{1,0},{2,1},{3,2},{5,4},{6,5},{7,6},{9,8},{10,9},{11,10},{13,12},{... | collective-permute-start | bytes 2064392 | tf_op jit(solution)/shard_map/ppermute | solution.py:299
  160.7 14.8 %collective-permute-start.13 = (bf16[128,2688]{1,0:T(8,128)(2,1)S(1)}, bf16[128,2688]{1,0:T(8,128)(2,1)S(1)}, u32[]{:S(2)}, u32[]{:S(2)}) collective-permute-start(bf16[128,2688]{1,0:T(8,128)(2,1)S(1)} %get-tuple-element.130), channel_id=1, source_target_pairs={{0,1},{1,2},{2,3},{4,5},{5,6},{6,7},{8,9},{9,10},{10,11},{12,13},{... | collective-permute-start | bytes 2064392 | tf_op jit(solution)/shard_map/ppermute | solution.py:299
  166.8 14.5 %collective-permute-start.12 = (bf16[128,2688]{1,0:T(8,128)(2,1)S(1)}, bf16[128,2688]{1,0:T(8,128)(2,1)S(1)}, u32[]{:S(2)}, u32[]{:S(2)}) collective-permute-start(bf16[128,2688]{1,0:T(8,128)(2,1)S(1)} %get-tuple-element.129), channel_id=1, source_target_pairs={{1,0},{2,1},{3,2},{5,4},{6,5},{7,6},{9,8},{10,9},{11,10},{13,12},{... | collective-permute-start | bytes 2064392 | tf_op jit(solution)/shard_map/ppermute | solution.py:299
  172.2 41.7 %copy-start.16 = (f32[256,1792]{1,0:T(8,128)}, f32[256,1792]{1,0:T(8,128)S(1)}, u32[]{:S(2)}) copy-start(f32[256,1792]{1,0:T(8,128)S(1)} %fusion.36.refs_2_.refs_3_.refs_4_.refs_5_) | copy-start | bytes 5505028
  176.8 15.7 %collective-permute-start.15 = (bf16[128,2688]{1,0:T(8,128)(2,1)}, bf16[128,2688]{1,0:T(8,128)(2,1)S(1)}, u32[]{:S(2)}, u32[]{:S(2)}) collective-permute-start(bf16[128,2688]{1,0:T(8,128)(2,1)} %get-tuple-element.136), channel_id=1, source_target_pairs={{0,1},{1,2},{2,3},{4,5},{5,6},{6,7},{8,9},{9,10},{10,11},{12,13},{... | collective-permute-start | bytes 2064392 | tf_op jit(solution)/shard_map/ppermute | solution.py:299
  182.6 15.1 %collective-permute-start.14 = (bf16[128,2688]{1,0:T(8,128)(2,1)}, bf16[128,2688]{1,0:T(8,128)(2,1)S(1)}, u32[]{:S(2)}, u32[]{:S(2)}) collective-permute-start(bf16[128,2688]{1,0:T(8,128)(2,1)} %get-tuple-element.135), channel_id=1, source_target_pairs={{1,0},{2,1},{3,2},{5,4},{6,5},{7,6},{9,8},{10,9},{11,10},{13,12},{... | collective-permute-start | bytes 2064392 | tf_op jit(solution)/shard_map/ppermute | solution.py:299
  193.1 15.1 %collective-permute-start.17 = (bf16[128,2688]{1,0:T(8,128)(2,1)S(1)}, bf16[128,2688]{1,0:T(8,128)(2,1)S(1)}, u32[]{:S(2)}, u32[]{:S(2)}) collective-permute-start(bf16[128,2688]{1,0:T(8,128)(2,1)S(1)} %get-tuple-element.142), channel_id=1, source_target_pairs={{0,1},{1,2},{2,3},{4,5},{5,6},{6,7},{8,9},{9,10},{10,11},{12,13},{... | collective-permute-start | bytes 2064392 | tf_op jit(solution)/shard_map/ppermute | solution.py:299
  198.8 15.1 %collective-permute-start.16 = (bf16[128,2688]{1,0:T(8,128)(2,1)S(1)}, bf16[128,2688]{1,0:T(8,128)(2,1)S(1)}, u32[]{:S(2)}, u32[]{:S(2)}) collective-permute-start(bf16[128,2688]{1,0:T(8,128)(2,1)S(1)} %get-tuple-element.141), channel_id=1, source_target_pairs={{1,0},{2,1},{3,2},{5,4},{6,5},{7,6},{9,8},{10,9},{11,10},{13,12},{... | collective-permute-start | bytes 2064392 | tf_op jit(solution)/shard_map/ppermute | solution.py:299
  208.8 13.3 %collective-permute-start.18 = (bf16[128,2688]{1,0:T(8,128)(2,1)S(1)}, bf16[128,2688]{1,0:T(8,128)(2,1)S(1)}, u32[]{:S(2)}, u32[]{:S(2)}) collective-permute-start(bf16[128,2688]{1,0:T(8,128)(2,1)S(1)} %get-tuple-element.148), channel_id=1, source_target_pairs={{0,1},{1,2},{2,3},{4,5},{5,6},{6,7},{8,9},{9,10},{10,11},{12,13},{... | collective-permute-start | bytes 2064392 | tf_op jit(solution)/shard_map/ppermute | solution.py:299
  215.0 13.1 %collective-permute-start.19 = (bf16[128,2688]{1,0:T(8,128)(2,1)S(1)}, bf16[128,2688]{1,0:T(8,128)(2,1)S(1)}, u32[]{:S(2)}, u32[]{:S(2)}) collective-permute-start(bf16[128,2688]{1,0:T(8,128)(2,1)S(1)} %get-tuple-element.147), channel_id=1, source_target_pairs={{1,0},{2,1},{3,2},{5,4},{6,5},{7,6},{9,8},{10,9},{11,10},{13,12},{... | collective-permute-start | bytes 2064392 | tf_op jit(solution)/shard_map/ppermute | solution.py:299
  242.9 224.6 %reduce-scatter.7.cloned.1.call-start = ((), (), s32[]{:S(2)}) async-start(), calls=%async_computation.9 | async-start | bytes 2359296 | tf_op jit(solution)/shard_map/reduce_scatter | solution.py:332
  243.0 23.8 %collective-permute-start.21 = (bf16[128,2688]{1,0:T(8,128)(2,1)}, bf16[128,2688]{1,0:T(8,128)(2,1)S(1)}, u32[]{:S(2)}, u32[]{:S(2)}) collective-permute-start(bf16[128,2688]{1,0:T(8,128)(2,1)} %get-tuple-element.152), channel_id=1, source_target_pairs={{0,1},{1,2},{2,3},{4,5},{5,6},{6,7},{8,9},{9,10},{10,11},{12,13},{... | collective-permute-start | bytes 2064392 | tf_op jit(solution)/shard_map/ppermute | solution.py:299
  244.3 28.8 %collective-permute-start.20 = (bf16[128,2688]{1,0:T(8,128)(2,1)}, bf16[128,2688]{1,0:T(8,128)(2,1)S(1)}, u32[]{:S(2)}, u32[]{:S(2)}) collective-permute-start(bf16[128,2688]{1,0:T(8,128)(2,1)} %copy-done.39), channel_id=1, source_target_pairs={{1,0},{2,1},{3,2},{5,4},{6,5},{7,6},{9,8},{10,9},{11,10},{13,12},{... | collective-permute-start | bytes 2064392 | tf_op jit(solution)/shard_map/ppermute | solution.py:299
  257.6 211.0 %reduce-scatter.13.cloned.1.call-start = ((), (), s32[]{:S(2)}) async-start(), calls=%async_computation.13 | async-start | bytes 2359296 | tf_op jit(solution)/shard_map/reduce_scatter | solution.py:332
  268.2 16.1 %collective-permute-start.23 = (bf16[128,2688]{1,0:T(8,128)(2,1)}, bf16[128,2688]{1,0:T(8,128)(2,1)S(1)}, u32[]{:S(2)}, u32[]{:S(2)}) collective-permute-start(bf16[128,2688]{1,0:T(8,128)(2,1)} %get-tuple-element.160), channel_id=1, source_target_pairs={{0,1},{1,2},{2,3},{4,5},{5,6},{6,7},{8,9},{9,10},{10,11},{12,13},{... | collective-permute-start | bytes 2064392 | tf_op jit(solution)/shard_map/ppermute | solution.py:299
  274.4 15.2 %collective-permute-start.22 = (bf16[128,2688]{1,0:T(8,128)(2,1)}, bf16[128,2688]{1,0:T(8,128)(2,1)S(1)}, u32[]{:S(2)}, u32[]{:S(2)}) collective-permute-start(bf16[128,2688]{1,0:T(8,128)(2,1)} %get-tuple-element.159), channel_id=1, source_target_pairs={{1,0},{2,1},{3,2},{5,4},{6,5},{7,6},{9,8},{10,9},{11,10},{13,12},{... | collective-permute-start | bytes 2064392 | tf_op jit(solution)/shard_map/ppermute | solution.py:299
  284.3 40.9 %copy-start.10 = (f32[256,1792]{1,0:T(8,128)}, f32[256,1792]{1,0:T(8,128)S(1)}, u32[]{:S(2)}) copy-start(f32[256,1792]{1,0:T(8,128)S(1)} %fusion.41.refs_2_.refs_3_.refs_4_.refs_5_) | copy-start | bytes 5505028
  284.9 38.7 %copy-start.34 = (bf16[128,2688]{1,0:T(8,128)(2,1)}, bf16[128,2688]{1,0:T(8,128)(2,1)S(1)}, u32[]{:S(2)}) copy-start(bf16[128,2688]{1,0:T(8,128)(2,1)S(1)} %get-tuple-element.166) | copy-start | bytes 2064388
  285.0 15.6 %collective-permute-start.25 = (bf16[128,2688]{1,0:T(8,128)(2,1)S(1)}, bf16[128,2688]{1,0:T(8,128)(2,1)S(1)}, u32[]{:S(2)}, u32[]{:S(2)}) collective-permute-start(bf16[128,2688]{1,0:T(8,128)(2,1)S(1)} %get-tuple-element.166), channel_id=1, source_target_pairs={{0,1},{1,2},{2,3},{4,5},{5,6},{6,7},{8,9},{9,10},{10,11},{12,13},{... | collective-permute-start | bytes 2064392 | tf_op jit(solution)/shard_map/ppermute | solution.py:299
  290.7 16.1 %collective-permute-start.24 = (bf16[128,2688]{1,0:T(8,128)(2,1)S(1)}, bf16[128,2688]{1,0:T(8,128)(2,1)S(1)}, u32[]{:S(2)}, u32[]{:S(2)}) collective-permute-start(bf16[128,2688]{1,0:T(8,128)(2,1)S(1)} %get-tuple-element.165), channel_id=1, source_target_pairs={{1,0},{2,1},{3,2},{5,4},{6,5},{7,6},{9,8},{10,9},{11,10},{13,12},{... | collective-permute-start | bytes 2064392 | tf_op jit(solution)/shard_map/ppermute | solution.py:299
  301.1 16.4 %collective-permute-start.26 = (bf16[128,2688]{1,0:T(8,128)(2,1)S(1)}, bf16[128,2688]{1,0:T(8,128)(2,1)S(1)}, u32[]{:S(2)}, u32[]{:S(2)}) collective-permute-start(bf16[128,2688]{1,0:T(8,128)(2,1)S(1)} %get-tuple-element.172), channel_id=1, source_target_pairs={{0,1},{1,2},{2,3},{4,5},{5,6},{6,7},{8,9},{9,10},{10,11},{12,13},{... | collective-permute-start | bytes 2064392 | tf_op jit(solution)/shard_map/ppermute | solution.py:299
  307.9 17.3 %collective-permute-start.27 = (bf16[128,2688]{1,0:T(8,128)(2,1)S(1)}, bf16[128,2688]{1,0:T(8,128)(2,1)S(1)}, u32[]{:S(2)}, u32[]{:S(2)}) collective-permute-start(bf16[128,2688]{1,0:T(8,128)(2,1)S(1)} %get-tuple-element.171), channel_id=1, source_target_pairs={{1,0},{2,1},{3,2},{5,4},{6,5},{7,6},{9,8},{10,9},{11,10},{13,12},{... | collective-permute-start | bytes 2064392 | tf_op jit(solution)/shard_map/ppermute | solution.py:299
  318.8 42.9 %collective-permute-start.29 = (bf16[128,2688]{1,0:T(8,128)(2,1)}, bf16[128,2688]{1,0:T(8,128)(2,1)S(1)}, u32[]{:S(2)}, u32[]{:S(2)}) collective-permute-start(bf16[128,2688]{1,0:T(8,128)(2,1)} %get-tuple-element.176), channel_id=1, source_target_pairs={{0,1},{1,2},{2,3},{4,5},{5,6},{6,7},{8,9},{9,10},{10,11},{12,13},{... | collective-permute-start | bytes 2064392 | tf_op jit(solution)/shard_map/ppermute | solution.py:299
  326.5 40.7 %collective-permute-start.28 = (bf16[128,2688]{1,0:T(8,128)(2,1)}, bf16[128,2688]{1,0:T(8,128)(2,1)S(1)}, u32[]{:S(2)}, u32[]{:S(2)}) collective-permute-start(bf16[128,2688]{1,0:T(8,128)(2,1)} %get-tuple-element.178), channel_id=1, source_target_pairs={{1,0},{2,1},{3,2},{5,4},{6,5},{7,6},{9,8},{10,9},{11,10},{13,12},{... | collective-permute-start | bytes 2064392 | tf_op jit(solution)/shard_map/ppermute | solution.py:299
  341.6 128.0 %reduce-scatter.11.cloned.1.call-start = ((), (), s32[]{:S(2)}) async-start(), calls=%async_computation.12 | async-start | bytes 2359296 | tf_op jit(solution)/shard_map/reduce_scatter | solution.py:332
  362.3 19.5 %collective-permute-start.31 = (bf16[128,2688]{1,0:T(8,128)(2,1)S(1)}, bf16[128,2688]{1,0:T(8,128)(2,1)S(1)}, u32[]{:S(2)}, u32[]{:S(2)}) collective-permute-start(bf16[128,2688]{1,0:T(8,128)(2,1)S(1)} %get-tuple-element.184), channel_id=1, source_target_pairs={{0,1},{1,2},{2,3},{4,5},{5,6},{6,7},{8,9},{9,10},{10,11},{12,13},{... | collective-permute-start | bytes 2064392 | tf_op jit(solution)/shard_map/ppermute | solution.py:299
  368.4 19.1 %collective-permute-start.30 = (bf16[128,2688]{1,0:T(8,128)(2,1)S(1)}, bf16[128,2688]{1,0:T(8,128)(2,1)S(1)}, u32[]{:S(2)}, u32[]{:S(2)}) collective-permute-start(bf16[128,2688]{1,0:T(8,128)(2,1)S(1)} %get-tuple-element.183), channel_id=1, source_target_pairs={{1,0},{2,1},{3,2},{5,4},{6,5},{7,6},{9,8},{10,9},{11,10},{13,12},{... | collective-permute-start | bytes 2064392 | tf_op jit(solution)/shard_map/ppermute | solution.py:299
  382.9 19.2 %collective-permute-start.33 = (bf16[128,2688]{1,0:T(8,128)(2,1)}, bf16[128,2688]{1,0:T(8,128)(2,1)S(1)}, u32[]{:S(2)}, u32[]{:S(2)}) collective-permute-start(bf16[128,2688]{1,0:T(8,128)(2,1)} %get-tuple-element.188), channel_id=1, source_target_pairs={{0,1},{1,2},{2,3},{4,5},{5,6},{6,7},{8,9},{9,10},{10,11},{12,13},{... | collective-permute-start | bytes 2064392 | tf_op jit(solution)/shard_map/ppermute | solution.py:299
  388.8 19.5 %collective-permute-start.32 = (bf16[128,2688]{1,0:T(8,128)(2,1)}, bf16[128,2688]{1,0:T(8,128)(2,1)S(1)}, u32[]{:S(2)}, u32[]{:S(2)}) collective-permute-start(bf16[128,2688]{1,0:T(8,128)(2,1)} %get-tuple-element.187), channel_id=1, source_target_pairs={{1,0},{2,1},{3,2},{5,4},{6,5},{7,6},{9,8},{10,9},{11,10},{13,12},{... | collective-permute-start | bytes 2064392 | tf_op jit(solution)/shard_map/ppermute | solution.py:299
  390.2 137.5 %reduce-scatter.17.cloned.1.call-start = ((), (), s32[]{:S(2)}) async-start(), calls=%async_computation.15 | async-start | bytes 2359296 | tf_op jit(solution)/shard_map/reduce_scatter | solution.py:332
  404.0 12.7 %collective-permute-start.34 = (bf16[128,2688]{1,0:T(8,128)(2,1)S(1)}, bf16[128,2688]{1,0:T(8,128)(2,1)S(1)}, u32[]{:S(2)}, u32[]{:S(2)}) collective-permute-start(bf16[128,2688]{1,0:T(8,128)(2,1)S(1)} %get-tuple-element.192), channel_id=1, source_target_pairs={{0,1},{1,2},{2,3},{4,5},{5,6},{6,7},{8,9},{9,10},{10,11},{12,13},{... | collective-permute-start | bytes 2064392 | tf_op jit(solution)/shard_map/ppermute | solution.py:299
  409.5 13.1 %collective-permute-start.35 = (bf16[128,2688]{1,0:T(8,128)(2,1)S(1)}, bf16[128,2688]{1,0:T(8,128)(2,1)S(1)}, u32[]{:S(2)}, u32[]{:S(2)}) collective-permute-start(bf16[128,2688]{1,0:T(8,128)(2,1)S(1)} %get-tuple-element.191), channel_id=1, source_target_pairs={{1,0},{2,1},{3,2},{5,4},{6,5},{7,6},{9,8},{10,9},{11,10},{13,12},{... | collective-permute-start | bytes 2064392 | tf_op jit(solution)/shard_map/ppermute | solution.py:299
  436.0 93.2 %reduce-scatter.15.cloned.1.call-start = ((), (), s32[]{:S(2)}) async-start(), calls=%async_computation.14 | async-start | bytes 2359296 | tf_op jit(solution)/shard_map/reduce_scatter | solution.py:332
  436.1 14.7 %collective-permute-start.39 = (bf16[128,896]{1,0:T(8,128)(2,1)S(1)}, bf16[128,896]{1,0:T(8,128)(2,1)S(1)}, u32[]{:S(2)}, u32[]{:S(2)}) collective-permute-start(bf16[128,896]{1,0:T(8,128)(2,1)S(1)} %get-tuple-element.194), channel_id=1, source_target_pairs={{0,1},{1,2},{2,3},{4,5},{5,6},{6,7},{8,9},{9,10},{10,11},{12,13},{... | collective-permute-start | bytes 688136 | tf_op jit(solution)/shard_map/ppermute | solution.py:299
  438.6 17.3 %collective-permute-start.36 = (bf16[128,896]{1,0:T(8,128)(2,1)S(1)}, bf16[128,896]{1,0:T(8,128)(2,1)S(1)}, u32[]{:S(2)}, u32[]{:S(2)}) collective-permute-start(bf16[128,896]{1,0:T(8,128)(2,1)S(1)} %get-tuple-element.196), channel_id=1, source_target_pairs={{1,0},{2,1},{3,2},{5,4},{6,5},{7,6},{9,8},{10,9},{11,10},{13,12},{... | collective-permute-start | bytes 688136 | tf_op jit(solution)/shard_map/ppermute | solution.py:299
  451.1 8.9 %collective-permute-start.40 = (bf16[128,896]{1,0:T(8,128)(2,1)S(1)}, bf16[128,896]{1,0:T(8,128)(2,1)S(1)}, u32[]{:S(2)}, u32[]{:S(2)}) collective-permute-start(bf16[128,896]{1,0:T(8,128)(2,1)S(1)} %shard_map.81), channel_id=1, source_target_pairs={{0,1},{1,2},{2,3},{4,5},{5,6},{6,7},{8,9},{9,10},{10,11},{12,13},{... | collective-permute-start | bytes 688136 | tf_op jit(solution)/shard_map/ppermute | solution.py:299
  456.2 8.6 %collective-permute-start.37 = (bf16[128,896]{1,0:T(8,128)(2,1)S(1)}, bf16[128,896]{1,0:T(8,128)(2,1)S(1)}, u32[]{:S(2)}, u32[]{:S(2)}) collective-permute-start(bf16[128,896]{1,0:T(8,128)(2,1)S(1)} %shard_map.79), channel_id=1, source_target_pairs={{1,0},{2,1},{3,2},{5,4},{6,5},{7,6},{9,8},{10,9},{11,10},{13,12},{... | collective-permute-start | bytes 688136 | tf_op jit(solution)/shard_map/ppermute | solution.py:299
  460.3 10.2 %collective-permute-start.41 = (bf16[128,896]{1,0:T(8,128)(2,1)S(1)}, bf16[128,896]{1,0:T(8,128)(2,1)S(1)}, u32[]{:S(2)}, u32[]{:S(2)}) collective-permute-start(bf16[128,896]{1,0:T(8,128)(2,1)S(1)} %shard_map.82), channel_id=1, source_target_pairs={{0,1},{1,2},{2,3},{4,5},{5,6},{6,7},{8,9},{9,10},{10,11},{12,13},{... | collective-permute-start | bytes 688136 | tf_op jit(solution)/shard_map/ppermute | solution.py:299
  465.2 11.0 %collective-permute-start.38 = (bf16[128,896]{1,0:T(8,128)(2,1)S(1)}, bf16[128,896]{1,0:T(8,128)(2,1)S(1)}, u32[]{:S(2)}, u32[]{:S(2)}) collective-permute-start(bf16[128,896]{1,0:T(8,128)(2,1)S(1)} %shard_map.80), channel_id=1, source_target_pairs={{1,0},{2,1},{3,2},{5,4},{6,5},{7,6},{9,8},{10,9},{11,10},{13,12},{... | collective-permute-start | bytes 688136 | tf_op jit(solution)/shard_map/ppermute | solution.py:299
  470.9 8.6 %collective-permute-start.42 = (bf16[128,896]{1,0:T(8,128)(2,1)S(1)}, bf16[128,896]{1,0:T(8,128)(2,1)S(1)}, u32[]{:S(2)}, u32[]{:S(2)}) collective-permute-start(bf16[128,896]{1,0:T(8,128)(2,1)S(1)} %shard_map.83), channel_id=1, source_target_pairs={{0,1},{1,2},{2,3},{4,5},{5,6},{6,7},{8,9},{9,10},{10,11},{12,13},{... | collective-permute-start | bytes 688136 | tf_op jit(solution)/shard_map/ppermute | solution.py:299
  490.0 10.4 %collective-permute-start.43 = (bf16[2,2,32,2048]{3,2,1,0:T(8,128)(2,1)S(1)}, bf16[2,2,32,2048]{3,2,1,0:T(8,128)(2,1)S(1)}, u32[]{:S(2)}, u32[]{:S(2)}) collective-permute-start(bf16[2,2,32,2048]{3,2,1,0:T(8,128)(2,1)S(1)} %fusion.18), channel_id=1, source_target_pairs={{0,8},{8,0},{16,24},{24,16},{1,9},{9,1},{17,25},{25,17},{2,10},{10... | collective-permute-start | bytes 1572872 | tf_op jit(solution)/shard_map/ppermute | solution.py:206
  500.0 2.0 collective-permute-start.46
  500.7 14.5 %collective-permute-start.44 = (bf16[1,2,32,2048]{3,2,1,0:T(8,128)(2,1)S(1)}, bf16[1,2,32,2048]{3,2,1,0:T(8,128)(2,1)S(1)}, u32[]{:S(2)}, u32[]{:S(2)}) collective-permute-start(bf16[1,2,32,2048]{3,2,1,0:T(8,128)(2,1)S(1)} %fusion.20), channel_id=1, source_target_pairs={{0,16},{8,24},{16,0},{24,8},{1,17},{9,25},{17,1},{25,9},{2,18},{10... | collective-permute-start | bytes 786440 | tf_op jit(solution)/shard_map/ppermute | solution.py:206
  502.2 18.0 %collective-permute-start.47 = (bf16[1,2,32,2048]{3,2,1,0:T(8,128)(2,1)S(1)}, bf16[1,2,32,2048]{3,2,1,0:T(8,128)(2,1)S(1)}, u32[]{:S(2)}, u32[]{:S(2)}) collective-permute-start(bf16[1,2,32,2048]{3,2,1,0:T(8,128)(2,1)S(1)} %fusion.21), channel_id=1, source_target_pairs={{0,16},{8,24},{16,0},{24,8},{1,17},{9,25},{17,1},{25,9},{2,18},{10... | collective-permute-start | bytes 786440 | tf_op jit(solution)/shard_map/ppermute | solution.py:206
  515.3 5.9 %collective-permute-start.45 = (bf16[1,32,2048]{2,1,0:T(8,128)(2,1)S(1)}, bf16[1,32,2048]{2,1,0:T(8,128)(2,1)S(1)}, u32[]{:S(2)}, u32[]{:S(2)}) collective-permute-start(bf16[1,32,2048]{2,1,0:T(8,128)(2,1)S(1)} %fusion.24), channel_id=1, source_target_pairs={{0,4},{4,0},{1,5},{5,1},{2,6},{6,2},{3,7},{7,3},{8,12},{12,8},{9,1... | collective-permute-start | bytes 393224 | tf_op jit(solution)/shard_map/ppermute | solution.py:206
  520.4 7.2 %collective-permute-start.48 = (bf16[1,32,2048]{2,1,0:T(8,128)(2,1)S(1)}, bf16[1,32,2048]{2,1,0:T(8,128)(2,1)S(1)}, u32[]{:S(2)}, u32[]{:S(2)}) collective-permute-start(bf16[1,32,2048]{2,1,0:T(8,128)(2,1)S(1)} %fusion.25), channel_id=1, source_target_pairs={{0,4},{4,0},{1,5},{5,1},{2,6},{6,2},{3,7},{7,3},{8,12},{12,8},{9,1... | collective-permute-start | bytes 393224 | tf_op jit(solution)/shard_map/ppermute | solution.py:206
  (81 other events, 940.9 us)
Sparse Core Ops, SparseCore 0:
  9.6 25.2 all-gather.4
  36.5 22.5 all-gather.6
  60.7 22.5 all-gather.8
  84.7 22.5 all-gather.10
  243.1 39.1 reduce-scatter.8
  285.8 41.2 reduce-scatter.6
  341.7 43.1 reduce-scatter.12
  390.3 42.8 reduce-scatter.10
  436.4 41.1 reduce-scatter.16
  481.2 48.0 reduce-scatter.14
